TPU v7x, 32 devices: a whole 2x2x4 slice. The times are simulated.
32 devices in a mesh: ta: 2 (over y), gz: 4 (over x, core), xy: 4 (over z).
Axes of the slice: x: 2, y: 2, z: 4, core: 2. Of those that a mesh axis runs over, the one named last changes fastest.
Arguments:
- right_side: float32 [2, 4, 4, 2, 32, 128], P('ta', 'gz', 'xy'), may hold values from -40 to 40
- stencil: float32 [2, 4, 4, 2, 9, 128, 128], P('ta', 'gz', 'xy'), may hold values from -0.5 to 1.5, as said below
- restrict: float32 [2, 4, 4, 2, 32, 128], P('ta', 'gz', 'xy'), may hold values from -0.5 to 0.5
- aggregate: int32 [2, 4, 4, 2], P('ta', 'gz', 'xy'), may hold values from 0 to 3, as said below
- coarsest_inverse: float32 [128, 128], P('xy'), may hold values from -0.5 to 0.5
Outputs:
- solution: float32 [2, 4, 4, 2, 32, 128], P('ta', 'gz', 'xy')
- residual: float32 [2, 4, 4, 2, 32, 128], P('ta', 'gz', 'xy')
Inputs may be any that keep to these rules, and one draw needn't show every extreme that they name: `aggregate`: sites are grouped into 2 x 2 x 2 x 2 blocks aligned at even coordinates; each block forms one coarsest site, and the coarsest sites are numbered in an order drawn from the seed. `stencil`: each self block is close to the identity; the other blocks are small and full.
All inputs are finite; a program needn't handle non-finite values.
Results may differ from a plain program's by a relative error of at most 0.0001.
Values sent between devices are 32-bit elements; how exact they have to be, the bound alone decides.
A program may use at most 64 MiB of HBM per device.

v0:
```python
import jax
import jax.numpy as jnp
from jax import lax
from jax.sharding import PartitionSpec as P


def extended(cells, sides, width):
    for axis, dim in sides:
        count = lax.axis_size(axis)
        head = lax.slice_in_dim(cells, 0, width, axis=dim)
        tail = lax.slice_in_dim(cells, cells.shape[dim] - width, cells.shape[dim], axis=dim)
        cells = jnp.concatenate(
            [
                lax.ppermute(tail, axis, [(i, (i + 1) % count) for i in range(count)]),
                cells,
                lax.ppermute(head, axis, [((i + 1) % count, i) for i in range(count)]),
            ],
            axis=dim,
        )
    return cells


def apply_operator(field, stencil):
    padded = extended(field, (("ta", 0), ("gz", 1), ("xy", 2)), 1)
    centre = field[0, 0, 0]
    stacked = jnp.stack(
        [
            centre,
            padded[2, 1, 1],
            padded[0, 1, 1],
            padded[1, 2, 1],
            padded[1, 0, 1],
            padded[1, 1, 2],
            padded[1, 1, 0],
            jnp.roll(centre, -1, 0),
            jnp.roll(centre, 1, 0),
        ],
        axis=1,
    )
    result = jnp.einsum(
        "xkij,xkrj->xri", stencil[0, 0, 0], stacked, precision=lax.Precision.HIGHEST
    )
    return result[None, None, None]


def inner_sum(one_side, other_side):
    return jnp.sum(one_side * other_side, axis=(0, 1, 2, 3, 5))


def body(right_side, stencil, restrict, aggregate, coarsest_inverse):
    image_first = apply_operator(right_side, stencil)
    cross_first, square_first = lax.psum(
        (inner_sum(image_first, right_side), inner_sum(image_first, image_first)),
        ("ta", "gz", "xy"),
    )
    step_first = cross_first / square_first
    resid_mid = right_side - step_first[:, None] * image_first
    image_raw = apply_operator(resid_mid, stencil)
    correlation_sum, cross_raw, square_raw, cross_old = lax.psum(
        (
            inner_sum(image_first, image_raw),
            inner_sum(image_raw, resid_mid),
            inner_sum(image_raw, image_raw),
            inner_sum(image_first, resid_mid),
        ),
        ("ta", "gz", "xy"),
    )
    beta = correlation_sum / square_first
    image_second = image_raw - beta[:, None] * image_first
    direction = resid_mid - beta[:, None] * right_side
    cross_second = cross_raw - beta * cross_old
    square_second = square_raw - beta * correlation_sum
    step_second = cross_second / square_second
    solution_gcr = step_first[:, None] * right_side + step_second[:, None] * direction
    residual = resid_mid - step_second[:, None] * image_second
    vectors = restrict[0, 0, 0]
    comps = vectors.shape[1]
    aggregates = coarsest_inverse.shape[1] // comps
    nrhs_count = residual.shape[4]
    restricted = jnp.einsum(
        "xkc,xrc->xrk", vectors, residual[0, 0, 0], precision=lax.Precision.HIGHEST
    )
    labels = aggregate[0, 0, 0]
    onehot = (labels[:, None] == jnp.arange(aggregates, dtype=jnp.int32)[None, :]).astype(
        jnp.float32
    )
    partial_rhs = jnp.einsum("xa,xrk->akr", onehot, restricted, precision=lax.Precision.HIGHEST)
    partial_rhs = partial_rhs.reshape(aggregates * comps, nrhs_count)
    coarse_rhs = lax.psum(partial_rhs, ("ta", "gz", "xy"))
    rows_part = jnp.dot(
        coarsest_inverse,
        coarse_rhs,
        precision=lax.Precision.HIGHEST,
        preferred_element_type=jnp.float32,
    )
    correction = lax.all_gather(rows_part, "xy", axis=0, tiled=True)
    correction = correction.reshape(aggregates, comps, nrhs_count)
    per_site = jnp.einsum("xa,akr->xkr", onehot, correction, precision=lax.Precision.HIGHEST)
    lifted = jnp.einsum("xkc,xkr->xrc", vectors, per_site, precision=lax.Precision.HIGHEST)
    solution = solution_gcr + lifted[None, None, None]
    return (solution, residual)


def solution(mesh):
    return jax.shard_map(
        body,
        mesh=mesh,
        in_specs=(
            P("ta", "gz", "xy", None, None, None),
            P("ta", "gz", "xy", None, None, None, None),
            P("ta", "gz", "xy", None, None, None),
            P("ta", "gz", "xy", None),
            P("xy", None),
        ),
        out_specs=(P("ta", "gz", "xy", None, None, None), P("ta", "gz", "xy", None, None, None)),
        check_vma=False,
    )
```

profile of v0, /device:TPU:0, one launch (start us, length us, event | category | flops | bytes accessed | tf_op | source)
XLA Modules:
  0.0 194.4 jit_solution(8783246398911059145)
XLA Ops:
  0.6 0.0 copy-start
  0.6 0.0 copy-start.1
  0.7 3.0 %collective-permute-start = (f32[1,1,1,2,32,128]{5,4,3,2,1,0:T(8,128)}, f32[1,1,1,2,32,128]{5,4,3,2,1,0:T(8,128)S(1)}, u32[]{:S(2)}, u32[]{:S(2)}) collective-permute-start(f32[1,1,1,2,32,128]{5,4,3,2,1,0:T(8,128)} %param.5), channel_id=1, source_target_pairs={{16,0},{0,16},{17,1},{1,17},{18,2},{2,18},{19,3},{3,19},{20,4},{4,... | collective-permute-start | bytes 98312 | tf_op jit(solution)/shard_map/ppermute | solution.py:16
  3.7 0.1 collective-permute-start.1
  3.8 0.8 constant_dynamic-update-slice_fusion.11
  4.6 0.7 slice_bitcast_fusion.11
  5.3 2.5 %collective-permute-done.1 = f32[1,1,1,2,32,128]{5,4,3,2,1,0:T(8,128)S(1)} collective-permute-done((f32[1,1,1,2,32,128]{5,4,3,2,1,0:T(8,128)}, f32[1,1,1,2,32,128]{5,4,3,2,1,0:T(8,128)S(1)}, u32[]{:S(2)}, u32[]{:S(2)}) %collective-permute-start.1) | collective-permute-done | bytes 32800 | tf_op jit(solution)/shard_map/ppermute | solution.py:14
  7.8 0.8 constant_dynamic-update-slice_fusion.1
  8.6 0.1 collective-permute-start.2
  8.7 0.5 collective-permute-start.3
  9.2 1.7 collective-permute-done.2
  10.9 2.9 %collective-permute-done.3 = f32[3,1,1,2,32,128]{5,4,3,2,1,0:T(8,128)S(1)} collective-permute-done((f32[3,1,1,2,32,128]{5,4,3,2,1,0:T(8,128)S(1)}, f32[3,1,1,2,32,128]{5,4,3,2,1,0:T(8,128)S(1)}, u32[]{:S(2)}, u32[]{:S(2)}) %collective-permute-start.3) | collective-permute-done | bytes 98336 | tf_op jit(solution)/shard_map/ppermute | solution.py:14
  13.8 3.7 %collective-permute-start.4 = (f32[3,3,1,2,32,128]{5,4,3,2,1,0:T(8,128)S(1)}, f32[3,3,1,2,32,128]{5,4,3,2,1,0:T(8,128)S(1)}, u32[]{:S(2)}, u32[]{:S(2)}) collective-permute-start(f32[3,3,1,2,32,128]{5,4,3,2,1,0:T(8,128)S(1)} %pad_maximum_fusion), channel_id=1, source_target_pairs={{1,0},{2,1},{3,2},{0,3},{5,4},{6,5},{7,6},{4,7},{9,8},{10,9},{11,1... | collective-permute-start | bytes 884744 | tf_op jit(solution)/shard_map/ppermute | solution.py:16
  17.5 7.4 %collective-permute-done.4 = f32[3,3,1,2,32,128]{5,4,3,2,1,0:T(8,128)S(1)} collective-permute-done((f32[3,3,1,2,32,128]{5,4,3,2,1,0:T(8,128)S(1)}, f32[3,3,1,2,32,128]{5,4,3,2,1,0:T(8,128)S(1)}, u32[]{:S(2)}, u32[]{:S(2)}) %collective-permute-start.4) | collective-permute-done | bytes 294944 | tf_op jit(solution)/shard_map/ppermute | solution.py:16
  24.9 6.3 %collective-permute-done.5 = f32[3,3,1,2,32,128]{5,4,3,2,1,0:T(8,128)S(1)} collective-permute-done((f32[3,3,1,2,32,128]{5,4,3,2,1,0:T(8,128)S(1)}, f32[3,3,1,2,32,128]{5,4,3,2,1,0:T(8,128)S(1)}, u32[]{:S(2)}, u32[]{:S(2)}) %collective-permute-start.5) | collective-permute-done | bytes 294944 | tf_op jit(solution)/shard_map/ppermute | solution.py:14
  31.3 1.4 fusion.10
  32.7 0.1 fusion.15
  32.8 39.4 %all-reduce.1 = (f32[32]{0:T(128)S(1)}, f32[32]{0:T(128)S(1)}) all-reduce(f32[32]{0:T(128)S(1)} %get-tuple-element.20, f32[32]{0:T(128)S(1)} %fusion.15), channel_id=1, replica_groups=mesh['ta'=2,'gz'=4,'xy'=4] {'ta','gz','xy'}, use_global_device_ids=true, to_apply=%region_1.2 | all-reduce | flops 64 | bytes 512 | tf_op jit(solution)/shard_map/psum | solution.py:52
  72.3 0.1 constant_dynamic-update-slice_fusion.20
  72.3 2.3 %collective-permute-start.6 = (f32[1,1,1,2,32,128]{5,4,3,2,1,0:T(8,128)S(1)}, f32[1,1,1,2,32,128]{5,4,3,2,1,0:T(8,128)S(1)}, u32[]{:S(2)}, u32[]{:S(2)}) collective-permute-start(f32[1,1,1,2,32,128]{5,4,3,2,1,0:T(8,128)S(1)} %get-tuple-element.15), channel_id=1, source_target_pairs={{16,0},{0,16},{17,1},{1,17},{18,2},{2,18},{19,3},{3,19},{20,4},{4,... | collective-permute-start | bytes 98312 | tf_op jit(solution)/shard_map/ppermute | solution.py:16
  74.6 0.1 collective-permute-start.7
  74.7 1.8 collective-permute-done.6
  76.5 2.0 %collective-permute-done.7 = f32[1,1,1,2,32,128]{5,4,3,2,1,0:T(8,128)S(1)} collective-permute-done((f32[1,1,1,2,32,128]{5,4,3,2,1,0:T(8,128)S(1)}, f32[1,1,1,2,32,128]{5,4,3,2,1,0:T(8,128)S(1)}, u32[]{:S(2)}, u32[]{:S(2)}) %collective-permute-start.7) | collective-permute-done | bytes 32800 | tf_op jit(solution)/shard_map/ppermute | solution.py:14
  78.5 0.1 collective-permute-start.8
  78.6 0.5 collective-permute-start.9
  79.1 2.7 %collective-permute-done.8 = f32[3,1,1,2,32,128]{5,4,3,2,1,0:T(8,128)S(1)} collective-permute-done((f32[3,1,1,2,32,128]{5,4,3,2,1,0:T(8,128)S(1)}, f32[3,1,1,2,32,128]{5,4,3,2,1,0:T(8,128)S(1)}, u32[]{:S(2)}, u32[]{:S(2)}) %collective-permute-start.8) | collective-permute-done | bytes 98336 | tf_op jit(solution)/shard_map/ppermute | solution.py:16
  81.8 0.9 collective-permute-done.9
  82.7 0.0 copy-start.3
  82.7 0.0 copy-start.5
  82.8 1.6 collective-permute-start.10
  84.3 0.5 collective-permute-start.11
  84.8 7.6 %collective-permute-done.10 = f32[3,3,1,2,32,128]{5,4,3,2,1,0:T(8,128)S(1)} collective-permute-done((f32[3,3,1,2,32,128]{5,4,3,2,1,0:T(8,128)S(1)}, f32[3,3,1,2,32,128]{5,4,3,2,1,0:T(8,128)S(1)}, u32[]{:S(2)}, u32[]{:S(2)}) %collective-permute-start.10) | collective-permute-done | bytes 294944 | tf_op jit(solution)/shard_map/ppermute | solution.py:16
  92.4 5.0 %collective-permute-done.11 = f32[3,3,1,2,32,128]{5,4,3,2,1,0:T(8,128)S(1)} collective-permute-done((f32[3,3,1,2,32,128]{5,4,3,2,1,0:T(8,128)S(1)}, f32[3,3,1,2,32,128]{5,4,3,2,1,0:T(8,128)S(1)}, u32[]{:S(2)}, u32[]{:S(2)}) %collective-permute-start.11) | collective-permute-done | bytes 294944 | tf_op jit(solution)/shard_map/ppermute | solution.py:14
  97.4 1.4 fusion.14
  98.8 0.1 fusion.11
  99.0 39.6 %all-reduce = (f32[32]{0:T(128)S(1)}, f32[32]{0:T(128)S(1)}, f32[32]{0:T(128)S(1)}, f32[32]{0:T(128)S(1)}) all-reduce(f32[32]{0:T(128)S(1)} %get-tuple-element.5, f32[32]{0:T(128)S(1)} %get-tuple-element.4, f32[32]{0:T(128)S(1)} %get-tuple-element.3, f32[32]{0:T(128)S(1)} %get-tuple-element.2), channel_id=1, replica_groups=mesh['ta'=2,'gz'=4,'xy'=4] {'ta','gz','xy'}, use_global_device_ids=true, to_apply=%region_7.8 | all-reduce | flops 128 | bytes 1024 | tf_op jit(solution)/shard_map/psum | solution.py:59
  138.6 0.1 bitcast_subtract_fusion
  138.7 0.0 copy-done.3
  138.7 0.0 copy-start.2
  138.7 0.2 fusion.7
  138.9 0.3 convolution_bitcast_fusion
  139.2 0.1 reshape.34
  139.3 40.6 %psum.55 = f32[128,32]{0,1:T(8,128)S(1)} all-reduce(f32[128,32]{0,1:T(8,128)S(1)} %reshape.34), channel_id=1, replica_groups=mesh['ta'=2,'gz'=4,'xy'=4] {'ta','gz','xy'}, use_global_device_ids=true, to_apply=%region_12.13 | all-reduce | flops 4096 | bytes 32768 | tf_op jit(solution)/shard_map/psum | solution.py:89
  179.9 0.1 convolution_bitcast_fusion.2
  180.0 0.1 copy.19
  180.1 13.1 %all_gather.3 = f32[128,32]{1,0:T(8,128)S(1)} all-gather(f32[32,32]{1,0:T(8,128)S(1)} %copy.19), channel_id=1, replica_groups=mesh['ta'=2,'gz'=4,'xy'=4] {'xy'}, dimensions={0}, use_global_device_ids=true | all-gather | bytes 20480 | tf_op jit(solution)/shard_map/all_gather | solution.py:96
  193.2 0.3 fusion.3
  193.5 0.9 fusion.2
  (32 shorter events, 0.2 us)
Async XLA Ops:
  0.6 30.6 %copy-start = (f32[1,1,1,2,9,128,128]{6,5,4,3,2,1,0:T(8,128)S(1)}, f32[1,1,1,2,9,128,128]{6,5,4,3,2,1,0:T(8,128)}, u32[]{:S(2)}) copy-start(f32[1,1,1,2,9,128,128]{6,5,4,3,2,1,0:T(8,128)} %param.6) | copy-start | bytes 3538948
  0.6 30.6 %copy-start.1 = (f32[1,1,1,2,32,128]{5,4,3,2,1,0:T(8,128)S(1)}, f32[1,1,1,2,32,128]{5,4,3,2,1,0:T(8,128)}, u32[]{:S(2)}) copy-start(f32[1,1,1,2,32,128]{5,4,3,2,1,0:T(8,128)} %param.5) | copy-start | bytes 98308
  0.7 7.9 %collective-permute-start = (f32[1,1,1,2,32,128]{5,4,3,2,1,0:T(8,128)}, f32[1,1,1,2,32,128]{5,4,3,2,1,0:T(8,128)S(1)}, u32[]{:S(2)}, u32[]{:S(2)}) collective-permute-start(f32[1,1,1,2,32,128]{5,4,3,2,1,0:T(8,128)} %param.5), channel_id=1, source_target_pairs={{16,0},{0,16},{17,1},{1,17},{18,2},{2,18},{19,3},{3,19},{20,4},{4,... | collective-permute-start | bytes 98312 | tf_op jit(solution)/shard_map/ppermute | solution.py:16
  3.7 4.1 %collective-permute-start.1 = (f32[1,1,1,2,32,128]{5,4,3,2,1,0:T(8,128)}, f32[1,1,1,2,32,128]{5,4,3,2,1,0:T(8,128)S(1)}, u32[]{:S(2)}, u32[]{:S(2)}) collective-permute-start(f32[1,1,1,2,32,128]{5,4,3,2,1,0:T(8,128)} %param.5), channel_id=1, source_target_pairs={{0,16},{16,0},{1,17},{17,1},{2,18},{18,2},{3,19},{19,3},{4,20},{20... | collective-permute-start | bytes 98312 | tf_op jit(solution)/shard_map/ppermute | solution.py:14
  8.6 2.3 %collective-permute-start.2 = (f32[3,1,1,2,32,128]{5,4,3,2,1,0:T(8,128)S(1)}, f32[3,1,1,2,32,128]{5,4,3,2,1,0:T(8,128)S(1)}, u32[]{:S(2)}, u32[]{:S(2)}) collective-permute-start(f32[3,1,1,2,32,128]{5,4,3,2,1,0:T(8,128)S(1)} %constant_dynamic-update-slice_fusion), channel_id=1, source_target_pairs={{4,0},{8,4},{12,8},{0,12},{5,1},{9,5},{13,9},{1,13},{6,2},{10,6},{... | collective-permute-start | bytes 294920 | tf_op jit(solution)/shard_map/ppermute | solution.py:16
  8.7 5.1 %collective-permute-start.3 = (f32[3,1,1,2,32,128]{5,4,3,2,1,0:T(8,128)S(1)}, f32[3,1,1,2,32,128]{5,4,3,2,1,0:T(8,128)S(1)}, u32[]{:S(2)}, u32[]{:S(2)}) collective-permute-start(f32[3,1,1,2,32,128]{5,4,3,2,1,0:T(8,128)S(1)} %constant_dynamic-update-slice_fusion), channel_id=1, source_target_pairs={{0,4},{4,8},{8,12},{12,0},{1,5},{5,9},{9,13},{13,1},{2,6},{6,10},{... | collective-permute-start | bytes 294920 | tf_op jit(solution)/shard_map/ppermute | solution.py:14
  13.8 11.1 %collective-permute-start.4 = (f32[3,3,1,2,32,128]{5,4,3,2,1,0:T(8,128)S(1)}, f32[3,3,1,2,32,128]{5,4,3,2,1,0:T(8,128)S(1)}, u32[]{:S(2)}, u32[]{:S(2)}) collective-permute-start(f32[3,3,1,2,32,128]{5,4,3,2,1,0:T(8,128)S(1)} %pad_maximum_fusion), channel_id=1, source_target_pairs={{1,0},{2,1},{3,2},{0,3},{5,4},{6,5},{7,6},{4,7},{9,8},{10,9},{11,1... | collective-permute-start | bytes 884744 | tf_op jit(solution)/shard_map/ppermute | solution.py:16
  17.5 13.8 %collective-permute-start.5 = (f32[3,3,1,2,32,128]{5,4,3,2,1,0:T(8,128)S(1)}, f32[3,3,1,2,32,128]{5,4,3,2,1,0:T(8,128)S(1)}, u32[]{:S(2)}, u32[]{:S(2)}) collective-permute-start(f32[3,3,1,2,32,128]{5,4,3,2,1,0:T(8,128)S(1)} %pad_maximum_fusion), channel_id=1, source_target_pairs={{0,1},{1,2},{2,3},{3,0},{4,5},{5,6},{6,7},{7,4},{8,9},{9,10},{10,1... | collective-permute-start | bytes 884744 | tf_op jit(solution)/shard_map/ppermute | solution.py:14
  72.3 4.2 %collective-permute-start.6 = (f32[1,1,1,2,32,128]{5,4,3,2,1,0:T(8,128)S(1)}, f32[1,1,1,2,32,128]{5,4,3,2,1,0:T(8,128)S(1)}, u32[]{:S(2)}, u32[]{:S(2)}) collective-permute-start(f32[1,1,1,2,32,128]{5,4,3,2,1,0:T(8,128)S(1)} %get-tuple-element.15), channel_id=1, source_target_pairs={{16,0},{0,16},{17,1},{1,17},{18,2},{2,18},{19,3},{3,19},{20,4},{4,... | collective-permute-start | bytes 98312 | tf_op jit(solution)/shard_map/ppermute | solution.py:16
  74.6 3.9 %collective-permute-start.7 = (f32[1,1,1,2,32,128]{5,4,3,2,1,0:T(8,128)S(1)}, f32[1,1,1,2,32,128]{5,4,3,2,1,0:T(8,128)S(1)}, u32[]{:S(2)}, u32[]{:S(2)}) collective-permute-start(f32[1,1,1,2,32,128]{5,4,3,2,1,0:T(8,128)S(1)} %get-tuple-element.15), channel_id=1, source_target_pairs={{0,16},{16,0},{1,17},{17,1},{2,18},{18,2},{3,19},{19,3},{4,20},{20... | collective-permute-start | bytes 98312 | tf_op jit(solution)/shard_map/ppermute | solution.py:14
  78.5 3.2 %collective-permute-start.8 = (f32[3,1,1,2,32,128]{5,4,3,2,1,0:T(8,128)S(1)}, f32[3,1,1,2,32,128]{5,4,3,2,1,0:T(8,128)S(1)}, u32[]{:S(2)}, u32[]{:S(2)}) collective-permute-start(f32[3,1,1,2,32,128]{5,4,3,2,1,0:T(8,128)S(1)} %pad_maximum_fusion.2), channel_id=1, source_target_pairs={{4,0},{8,4},{12,8},{0,12},{5,1},{9,5},{13,9},{1,13},{6,2},{10,6},{... | collective-permute-start | bytes 294920 | tf_op jit(solution)/shard_map/ppermute | solution.py:16
  78.6 4.1 %collective-permute-start.9 = (f32[3,1,1,2,32,128]{5,4,3,2,1,0:T(8,128)S(1)}, f32[3,1,1,2,32,128]{5,4,3,2,1,0:T(8,128)S(1)}, u32[]{:S(2)}, u32[]{:S(2)}) collective-permute-start(f32[3,1,1,2,32,128]{5,4,3,2,1,0:T(8,128)S(1)} %pad_maximum_fusion.2), channel_id=1, source_target_pairs={{0,4},{4,8},{8,12},{12,0},{1,5},{5,9},{9,13},{13,1},{2,6},{6,10},{... | collective-permute-start | bytes 294920 | tf_op jit(solution)/shard_map/ppermute | solution.py:14
  82.7 55.9 %copy-start.3 = (f32[1,1,1,2,32,128]{5,4,3,2,1,0:T(8,128)S(1)}, f32[1,1,1,2,32,128]{5,4,3,2,1,0:T(8,128)}, u32[]{:S(2)}) copy-start(f32[1,1,1,2,32,128]{5,4,3,2,1,0:T(8,128)} %param.7) | copy-start | bytes 98308
  82.7 56.1 %copy-start.5 = (s32[1,1,1,2]{3,2,1,0:T(1,128)S(1)}, s32[1,1,1,2]{3,2,1,0:T(1,128)}, u32[]{:S(2)}) copy-start(s32[1,1,1,2]{3,2,1,0:T(1,128)} %param.8) | copy-start | bytes 28
  82.8 9.7 %collective-permute-start.10 = (f32[3,3,1,2,32,128]{5,4,3,2,1,0:T(8,128)S(1)}, f32[3,3,1,2,32,128]{5,4,3,2,1,0:T(8,128)S(1)}, u32[]{:S(2)}, u32[]{:S(2)}) collective-permute-start(f32[3,3,1,2,32,128]{5,4,3,2,1,0:T(8,128)S(1)} %pad_maximum_fusion.1), channel_id=1, source_target_pairs={{1,0},{2,1},{3,2},{0,3},{5,4},{6,5},{7,6},{4,7},{9,8},{10,9},{11,1... | collective-permute-start | bytes 884744 | tf_op jit(solution)/shard_map/ppermute | solution.py:16
  84.3 13.1 %collective-permute-start.11 = (f32[3,3,1,2,32,128]{5,4,3,2,1,0:T(8,128)S(1)}, f32[3,3,1,2,32,128]{5,4,3,2,1,0:T(8,128)S(1)}, u32[]{:S(2)}, u32[]{:S(2)}) collective-permute-start(f32[3,3,1,2,32,128]{5,4,3,2,1,0:T(8,128)S(1)} %pad_maximum_fusion.1), channel_id=1, source_target_pairs={{0,1},{1,2},{2,3},{3,0},{4,5},{5,6},{6,7},{7,4},{8,9},{9,10},{10,1... | collective-permute-start | bytes 884744 | tf_op jit(solution)/shard_map/ppermute | solution.py:14
  92.4 87.5 %copy-start.4 = (f32[32,128]{1,0:T(8,128)S(1)}, f32[32,128]{1,0:T(8,128)}, u32[]{:S(2)}) copy-start(f32[32,128]{1,0:T(8,128)} %param.9) | copy-start | bytes 49156
  138.7 55.7 %copy-start.2 = (f32[1,1,1,2,32,128]{5,4,3,2,1,0:T(8,128)}, f32[1,1,1,2,32,128]{5,4,3,2,1,0:T(8,128)S(1)}, u32[]{:S(2)}) copy-start(f32[1,1,1,2,32,128]{5,4,3,2,1,0:T(8,128)S(1)} %bitcast_subtract_fusion) | copy-start | bytes 98308
where the time goes:
time: 195 us; the launch traced here: 194 us
  blocking collectives  133 us (68%)
  waiting for transfers between devices  40.8 us (21%)
  starting transfers between devices  12.3 us (6%)
  matrix products  4.6 us (2%)
  local copies, waits for them, and re-layouts  2.55 us (1%)
    psum x1, blocking collectives, body(): coarse_rhs = lax.psum(partial_rhs, ('ta', 'gz', 'xy'))  40.6 us
    psum x1, blocking collectives, body(): lax.psum((inner_sum(image_first, image_raw), inner_sum(image_raw, resid_m...  39.6 us
    psum x1, blocking collectives, body(): lax.psum((inner_sum(image_first, right_side), inner_sum(image_first, imag...  39.4 us
    ppermute x6, waiting for transfers between devices, extended(): lax.ppermute(head, axis, [((i + 1) % count, i) for i in range(count)])  21.2 us
    ppermute x6, waiting for transfers between devices, extended(): lax.ppermute(tail, axis, [(i, (i + 1) % count) for i in range(count)])  19.7 us
    all_gather x1, blocking collectives, body(): correction = lax.all_gather(rows_part, 'xy', axis=0, tiled=True)  13.1 us
    ppermute x6, starting transfers between devices, extended(): lax.ppermute(head, axis, [((i + 1) % count, i) for i in range(count)])  10.6 us
  transfers between devices with their start and end apart: 12, of which 11 were waited for; matrix products, arithmetic and copies ran while one was open for 1% of the time, Pallas kernels for 0%

commit v1 on v0

v1 whole, which is shorter than its diff:
```python
import functools
import itertools

import jax
import jax.numpy as jnp
from jax import lax
from jax.experimental import pallas as pl
from jax.experimental.pallas import tpu as pltpu
from jax.sharding import PartitionSpec as P

AXES = ("ta", "gz", "xy")
F32 = jnp.float32
BF16 = jnp.bfloat16
MESH = pl.DeviceIdType.MESH


def split(x):
    high = x.astype(BF16)
    return high, (x - high.astype(F32)).astype(BF16)


def dot_nt(a, b):
    return lax.dot_general(a, b, (((1,), (1,)), ((), ())), preferred_element_type=F32)


def dot_nn(a, b):
    return lax.dot_general(a, b, (((1,), (0,)), ((), ())), preferred_element_type=F32)


def stack_split(x):
    return jnp.concatenate(split(x), axis=0)


def fold(o):
    r, n = o.shape[0] // 2, o.shape[1] // 2
    return o[:r, :n] + (o[:r, n:] + o[r:, :n])


def loop(n, step, init, most=8):
    if n <= most:
        for i in range(n):
            init = step(i, init)
        return init
    return lax.fori_loop(0, n, step, init)


def kernel(
    sizes, agg_ref, b_ref, sten_ref, res_ref, inv_ref, sol_ref, resid_ref,
    sten, sw, rp, halo1, halo2, w1, w2, inv, lab, wr, near, far,
    sten_sem, h1s, h1r, h2s, h2r, ivs, ivr, lbs, lbr, nrs, nrr, frs, frr,
):
    xs, nrhs, comps = b_ref.shape
    k3 = res_ref.shape[1]
    na, _, nc3 = inv.shape
    per = inv_ref.shape[0]
    groups = far.shape[0]
    me = tuple(lax.axis_index(a) for a in AXES)

    def at(offset):
        return {a: lax.rem(i + o, n) for a, i, o, n in zip(AXES, me, offset, sizes)}

    def across(bits):
        return {a: (i + 1 - 2 * lax.rem(i, 2)) if f else i for a, i, f in zip(AXES, me, bits)}

    def line(axis, o):
        return tuple(o if a == axis else 0 for a in range(3))

    halo_sends = []
    for a in range(3):
        halo_sends.append((2 * a, line(a, sizes[a] - 1)))
        if sizes[a] > 2:
            halo_sends.append((2 * a + 1, line(a, 1)))
    near_sends = [bits for bits in itertools.product((0, 1), repeat=3) if any(bits)]
    far_sends = [
        tuple(2 * o for o in offs)
        for offs in itertools.product(*(range(n // 2) for n in sizes))
        if any(offs)
    ]
    inv_sends = [line(2, o) for o in range(1, sizes[2])]

    copies = [
        pltpu.make_async_copy(sten_ref.at[x], sten.at[x], sten_sem.at[x]) for x in range(xs)
    ]
    for c in copies:
        c.start()

    barrier = pltpu.get_barrier_semaphore()
    offsets = sorted({o for _, o in halo_sends} | set(far_sends) | set(inv_sends))
    diagonals = [bits for bits in near_sends if sum(bits) > 1]
    for device in [at(o) for o in offsets] + [across(f) for f in diagonals]:
        pl.semaphore_signal(barrier, inc=1, device_id=device, device_id_type=MESH)

    lab[0] = jnp.full(lab.shape[1:], agg_ref[0].astype(F32), F32)
    inv[pl.ds(me[2] * per, per)] = inv_ref[...]
    rp[...] = jnp.zeros_like(rp)
    for x in range(xs):
        high, low = split(res_ref[x])
        for f in range(3):
            cols = pl.ds((f * xs + x) * comps, comps)
            rp[pl.ds(f * k3, k3), cols] = high
            rp[pl.ds(comps + f * k3, k3), cols] = low

    pl.semaphore_wait(barrier, len(offsets) + len(diagonals))

    def remote(src, dst, send, recv, device):
        return pltpu.make_async_remote_copy(
            src_ref=src, dst_ref=dst, send_sem=send, recv_sem=recv,
            device_id=device, device_id_type=MESH,
        )

    def start_halo(src, halo, send, recv):
        out = [remote(src, halo.at[s], send.at[s], recv.at[s], at(o)) for s, o in halo_sends]
        for c in out:
            c.start()
        return out

    first = start_halo(b_ref, halo1, h1s, h1r)
    early = [
        remote(inv_ref, inv.at[pl.ds(me[2] * per, per)], ivs.at[i], ivr.at[i], at(o))
        for i, o in enumerate(inv_sends)
    ] + [
        remote(lab.at[0], lab.at[i + 1], lbs.at[i], lbr.at[i], at(o))
        for i, o in enumerate(far_sends)
    ]
    for c in early:
        c.start()

    for x in range(xs):
        copies[x].wait()
        for k in range(9):
            high, low = split(sten[x, k])
            cols = pl.ds(k * comps, comps)
            sw[x, pl.ds(0, comps), cols] = high
            sw[x, pl.ds(comps, comps), cols] = low

    def local_part(field):
        out = []
        for x in range(xs):
            ahead = jnp.concatenate([field[(x + 1) % xs], field[(x + xs - 1) % xs]], axis=1)
            out.append(
                fold(dot_nt(stack_split(field[x]), sw[x, :, pl.ds(0, comps)]))
                + fold(dot_nt(stack_split(ahead), sw[x, :, pl.ds(7 * comps, 2 * comps)]))
            )
        return out

    def halo_part(halo, base):
        out = []
        for x in range(xs):
            sides = []
            for a in range(3):
                sides.append(halo[2 * a, x])
                sides.append(halo[2 * a + (1 if sizes[a] > 2 else 0), x])
            lhs = stack_split(jnp.concatenate(sides, axis=1))
            out.append(base[x] + fold(dot_nt(lhs, sw[x, :, pl.ds(comps, 6 * comps)])))
        return out

    def restricted(field, f):
        lhs = jnp.concatenate(field, axis=1)
        cols = pl.ds(f * xs * comps, xs * comps)
        return fold(dot_nt(stack_split(lhs), rp[:, cols]))

    lane = lax.broadcasted_iota(jnp.int32, (nrhs, comps), 1)

    def product(u, v, i):
        total = sum(u[x] * v[x] for x in range(xs))
        total = jnp.sum(total, axis=1, keepdims=True)
        return jnp.where(lane == 3 * k3 + i, total, 0.0)

    bs = [b_ref[x] for x in range(xs)]
    base = local_part(bs)
    message = restricted(bs, 0)
    for c in first:
        c.wait_recv()
    w1s = halo_part(halo1, base)
    for x in range(xs):
        w1[x] = w1s[x]
    second = start_halo(w1, halo2, h2s, h2r)

    base = local_part(w1s)
    message = message + restricted(w1s, 1) + product(w1s, w1s, 0) + product(w1s, bs, 1)
    for c in early:
        c.wait_recv()

    own = inv[agg_ref[0]]
    own_high, own_low = split(own)
    rows = lax.broadcasted_iota(jnp.int32, (comps, nc3), 0)
    cols = lax.broadcasted_iota(jnp.int32, (comps, nc3), 1)
    same = (lax.rem(rows, k3) == lax.rem(cols, k3)) & (rows < 3 * k3)
    block = (cols // k3).astype(F32)
    vec_high, vec_low = split(jnp.concatenate([res_ref[x] for x in range(xs)], axis=1))

    def prepare(g, carry):
        label = lab[g][0:1, 0:1]
        pick = jnp.where(same & (block == label), 1.0, 0.0).astype(BF16)
        weights = dot_nt(pick, own_high) + dot_nt(pick, own_low)
        high, low = split(weights)
        lift = dot_nn(high, vec_high) + (dot_nn(high, vec_low) + dot_nn(low, vec_high))
        high, low = split(lift)
        width = xs * comps
        wr[g, :, pl.ds(0, width)] = high
        wr[g, :, pl.ds(width, width)] = low
        return carry

    loop(groups, prepare, 0)

    for c in second:
        c.wait_recv()
    w2s = halo_part(halo2, base)
    message = message + (
        restricted(w2s, 2)
        + (product(w1s, w2s, 2) + product(w2s, w2s, 3) + product(w2s, bs, 4))
    )
    near[0] = message
    third = [
        remote(near.at[0], near.at[i + 1], nrs.at[i], nrr.at[i], across(f))
        for i, f in enumerate(near_sends)
    ]
    for c in third:
        c.start()
    for x in range(xs):
        w2[x] = w2s[x]
    for c in third:
        c.wait_recv()
    total = message
    for i in range(len(near_sends)):
        total = total + near[i + 1]
    far[0] = total
    fourth = [
        remote(far.at[0], far.at[i + 1], frs.at[i], frr.at[i], at(o))
        for i, o in enumerate(far_sends)
    ]
    for c in fourth:
        c.start()
    for c in first + early + second + third:
        c.wait_send()
    for c in fourth:
        c.wait_recv()

    sums = loop(groups, lambda g, acc: acc + far[g], jnp.zeros((nrhs, comps), F32))
    square, cross, corr, square2, cross2 = (
        sums[:, 3 * k3 + i : 3 * k3 + i + 1] for i in range(5)
    )
    step = cross / square
    ratio = corr / square
    turn = (step * corr - cross2) / (square2 - ratio * corr)
    push = step + turn * ratio
    weight = jnp.where(
        lane < k3, 1.0, jnp.where(lane < 2 * k3, -push, jnp.where(lane < 3 * k3, turn, 0.0))
    )
    width = xs * comps

    def lift_step(g, acc):
        return acc + dot_nn(stack_split(far[g] * weight), wr[g])

    lifted = fold(loop(groups, lift_step, jnp.zeros((2 * nrhs, 2 * width), F32)))
    for x in range(xs):
        bx, ux, vx = b_ref[x], w1[x], w2[x]
        resid_ref[x] = bx - push * ux + turn * vx
        sol_ref[x] = (push * bx - turn * ux) + lifted[:, x * comps : (x + 1) * comps]
    for c in fourth:
        c.wait_send()


def body(sizes, right_side, stencil, restrict, aggregate, coarsest_inverse):
    shape = right_side.shape
    xs, nrhs, comps = shape[3:]
    k3 = restrict.shape[4]
    nc3 = coarsest_inverse.shape[1]
    na = nc3 // k3
    groups = (sizes[0] // 2) * (sizes[1] // 2) * (sizes[2] // 2)
    per = coarsest_inverse.shape[0] // k3
    vmem = pl.BlockSpec(memory_space=pltpu.VMEM)
    dma = pltpu.SemaphoreType.DMA
    field = jax.ShapeDtypeStruct((xs, nrhs, comps), F32)
    sol, resid = pl.pallas_call(
        functools.partial(kernel, sizes),
        out_shape=(field, field),
        in_specs=[
            pl.BlockSpec(memory_space=pltpu.SMEM),
            vmem,
            pl.BlockSpec(memory_space=pl.ANY),
            vmem,
            vmem,
        ],
        out_specs=(vmem, vmem),
        scratch_shapes=[
            pltpu.VMEM((xs, 9, comps, comps), F32),
            pltpu.VMEM((xs, 2 * comps, 9 * comps), BF16),
            pltpu.VMEM((2 * comps, 3 * xs * comps), BF16),
            pltpu.VMEM((6, xs, nrhs, comps), F32),
            pltpu.VMEM((6, xs, nrhs, comps), F32),
            pltpu.VMEM((xs, nrhs, comps), F32),
            pltpu.VMEM((xs, nrhs, comps), F32),
            pltpu.VMEM((na, k3, nc3), F32),
            pltpu.VMEM((groups, 8, comps), F32),
            pltpu.VMEM((groups, comps, 2 * xs * comps), BF16),
            pltpu.VMEM((8, nrhs, comps), F32),
            pltpu.VMEM((groups, nrhs, comps), F32),
            dma((xs,)),
            dma((6,)), dma((6,)), dma((6,)), dma((6,)),
            dma((sizes[2],)), dma((sizes[2],)),
            dma((groups,)), dma((groups,)),
            dma((7,)), dma((7,)),
            dma((groups,)), dma((groups,)),
        ],
        compiler_params=pltpu.CompilerParams(
            collective_id=0,
            has_side_effects=True,
            vmem_limit_bytes=(16 if groups <= 8 else 48) * 2**20,
        ),
    )(
        aggregate.reshape(xs),
        right_side.reshape(xs, nrhs, comps),
        stencil.reshape(xs, 9, comps, comps),
        restrict.reshape(xs, k3, comps),
        coarsest_inverse.reshape(per, k3, nc3),
    )
    return sol.reshape(shape), resid.reshape(shape)


def solution(mesh):
    sizes = tuple(mesh.shape[a] for a in AXES)
    return jax.shard_map(
        functools.partial(body, sizes),
        mesh=mesh,
        in_specs=(
            P("ta", "gz", "xy", None, None, None),
            P("ta", "gz", "xy", None, None, None, None),
            P("ta", "gz", "xy", None, None, None),
            P("ta", "gz", "xy", None),
            P("xy", None),
        ),
        out_specs=(P("ta", "gz", "xy", None, None, None), P("ta", "gz", "xy", None, None, None)),
        check_vma=False,
    )
```

time: 195 us -> 30.4 us (0.16)
  blocking collectives: 133 us -> 0 us
  waiting for transfers between devices: 40.8 us -> 0 us
  Pallas kernels: 0 us -> 24 us
  starting transfers between devices: 12.3 us -> 0 us
  matrix products: 4.6 us -> 0 us
  local copies, waits for them, and re-layouts: 2.55 us -> 5.38 us
    psum x3 -> x0, blocking collectives: 120 us -> none  [the longest x1 40.6 us: body(): coarse_rhs = lax.psum(partial_rhs, ('ta', 'gz', 'xy'))]
    ppermute x12 -> x0, waiting for transfers between devices: 40.8 us -> none  [the longest x6 21.2 us: extended(): lax.ppermute(head, axis, [((i + 1) % count, i) for i in range(count)])]
    pallas_call x0 -> x1, Pallas kernels: none -> 24 us  [body(): pl.pallas_call(functools.partial(kernel, sizes), out_shape=(field, field)...]
    all_gather x1 -> x0, blocking collectives: 13.1 us -> none  [body(): correction = lax.all_gather(rows_part, 'xy', axis=0, tiled=True)]
    ppermute x12 -> x0, starting transfers between devices: 12.3 us -> none  [the longest x6 10.6 us: extended(): lax.ppermute(head, axis, [((i + 1) % count, i) for i in range(count)])]
    dot_general x7 -> x0, matrix products: 4.6 us -> none  [the longest x2 2.86 us: apply_operator(): jnp.einsum('xkij,xkrj->xri', stencil[0, 0, 0], stacked, precision=lax.Pre...]
    unnamed x27 -> x12, local copies, waits for them, and re-layouts: 1.65 us -> 5.38 us
  transfers between devices with their start and end apart: 12 -> 0, of which waited for: 11 -> 0; matrix products, arithmetic and copies ran while one was open for 1% -> 0% of each run, Pallas kernels for 0% -> 0%
where the time goes in v1:
time: 30.4 us; the launch traced here: 30 us
  Pallas kernels  24 us (79%)
  local copies, waits for them, and re-layouts  5.38 us (18%)
  between operations  0.65 us (2%)
    pallas_call x1, Pallas kernels, body(): pl.pallas_call(functools.partial(kernel, sizes), out_shape=(field, field)...  24 us
    unnamed x12, local copies, waits for them, and re-layouts  5.38 us

profile of v1, /device:TPU:0, one launch (start us, length us, event | category | flops | bytes accessed | tf_op | source)
XLA Modules:
  0.0 30.0 jit_solution(4757806212523942680)
XLA Ops:
  0.6 0.0 copy-start
  0.6 1.3 %copy-done = f32[1,1,1,2,9,128,128]{6,5,4,3,2,1,0:T(8,128)S(1)} copy-done((f32[1,1,1,2,9,128,128]{6,5,4,3,2,1,0:T(8,128)S(1)}, f32[1,1,1,2,9,128,128]{6,5,4,3,2,1,0:T(8,128)}, u32[]{:S(2)}) %copy-start) | copy-done | bytes 1179672
  1.9 0.0 copy-start.1
  1.9 0.8 %copy-done.1 = f32[1,1,1,2,32,128]{5,4,3,2,1,0:T(8,128)S(1)} copy-done((f32[1,1,1,2,32,128]{5,4,3,2,1,0:T(8,128)S(1)}, f32[1,1,1,2,32,128]{5,4,3,2,1,0:T(8,128)}, u32[]{:S(2)}) %copy-start.1) | copy-done | bytes 32792
  2.7 0.0 copy-start.2
  2.7 0.8 %copy-done.2 = f32[1,1,1,2,32,128]{5,4,3,2,1,0:T(8,128)S(1)} copy-done((f32[1,1,1,2,32,128]{5,4,3,2,1,0:T(8,128)S(1)}, f32[1,1,1,2,32,128]{5,4,3,2,1,0:T(8,128)}, u32[]{:S(2)}) %copy-start.2) | copy-done | bytes 32792
  3.4 0.0 copy-start.3
  3.4 0.7 %copy-done.3 = f32[32,128]{1,0:T(8,128)S(1)} copy-done((f32[32,128]{1,0:T(8,128)S(1)}, f32[32,128]{1,0:T(8,128)}, u32[]{:S(2)}) %copy-start.3) | copy-done | bytes 16408
  4.1 0.0 copy-start.4
  4.1 0.7 %copy-done.4 = s32[1,1,1,2]{3,2,1,0:T(1,128)S(1)} copy-done((s32[1,1,1,2]{3,2,1,0:T(1,128)S(1)}, s32[1,1,1,2]{3,2,1,0:T(1,128)}, u32[]{:S(2)}) %copy-start.4) | copy-done | bytes 32
  4.8 24.0 %shard_map.68 = (f32[2,32,128]{2,1,0:T(8,128)S(1)}, f32[2,32,128]{2,1,0:T(8,128)S(1)}) custom-call(s32[2]{0:T(128)S(1)} %bitcast.13, f32[2,32,128]{2,1,0:T(8,128)S(1)} %bitcast.8, f32[2,9,128,128]{3,2,1,0:T(8,128)S(1)} %bitcast.7, f32[2,32,128]{2,1,0:T(8,128)S(1)} %bitcast.9, f32[1,32,128]{2,1,0:T(8,128)S(1)} %bitcast.12), custom_call_target="tpu_custom_call" | custom-call | tf_op jit(solution)/shard_map/pallas_call | solution.py:275
  28.8 0.6 %copy.9 = f32[1,1,1,2,32,128]{5,4,3,2,1,0:T(8,128)} copy(f32[1,1,1,2,32,128]{5,4,3,2,1,0:T(8,128)S(1)} %bitcast.11) | data formatting | bytes 65536
  29.4 0.6 %copy.10 = f32[1,1,1,2,32,128]{5,4,3,2,1,0:T(8,128)} copy(f32[1,1,1,2,32,128]{5,4,3,2,1,0:T(8,128)S(1)} %bitcast.10) | data formatting | bytes 65536
Async XLA Ops:
  0.6 1.3 %copy-start = (f32[1,1,1,2,9,128,128]{6,5,4,3,2,1,0:T(8,128)S(1)}, f32[1,1,1,2,9,128,128]{6,5,4,3,2,1,0:T(8,128)}, u32[]{:S(2)}) copy-start(f32[1,1,1,2,9,128,128]{6,5,4,3,2,1,0:T(8,128)} %param.6) | copy-start | bytes 3538948
  1.9 0.8 %copy-start.1 = (f32[1,1,1,2,32,128]{5,4,3,2,1,0:T(8,128)S(1)}, f32[1,1,1,2,32,128]{5,4,3,2,1,0:T(8,128)}, u32[]{:S(2)}) copy-start(f32[1,1,1,2,32,128]{5,4,3,2,1,0:T(8,128)} %param.5) | copy-start | bytes 98308
  2.7 0.8 %copy-start.2 = (f32[1,1,1,2,32,128]{5,4,3,2,1,0:T(8,128)S(1)}, f32[1,1,1,2,32,128]{5,4,3,2,1,0:T(8,128)}, u32[]{:S(2)}) copy-start(f32[1,1,1,2,32,128]{5,4,3,2,1,0:T(8,128)} %param.7) | copy-start | bytes 98308
  3.4 0.7 %copy-start.3 = (f32[32,128]{1,0:T(8,128)S(1)}, f32[32,128]{1,0:T(8,128)}, u32[]{:S(2)}) copy-start(f32[32,128]{1,0:T(8,128)} %param.9) | copy-start | bytes 49156
  4.1 0.7 %copy-start.4 = (s32[1,1,1,2]{3,2,1,0:T(1,128)S(1)}, s32[1,1,1,2]{3,2,1,0:T(1,128)}, u32[]{:S(2)}) copy-start(s32[1,1,1,2]{3,2,1,0:T(1,128)} %param.8) | copy-start | bytes 28
